TPU v7x, 256 devices: a whole 4x4x8 slice. The times are simulated.
256 devices in a mesh: row: 8 (over y, core), col: 32 (over z, x).
Axes of the slice: x: 4, y: 4, z: 8, core: 2. Of those that a mesh axis runs over, the one named last changes fastest.
Arguments:
- root_inverse: bfloat16 [8192, 8192], P('row', 'col'), may hold values from -1 to 2, as said below
- child_inverse: bfloat16 [2, 4096, 4096], P(None, 'row', 'col'), may hold values from -1 to 2, as said below
- child_panel: bfloat16 [2, 1024, 4096], P(None, 'row', 'col'), may hold values from -0.1875 to 0.1875
- ancestors: int32 [2, 8], replicated, may hold values from 0 to 63, as said below
Outputs:
- root_block: float32 [8192, 8192], P('row', 'col')
- cross_block: float32 [2, 1024, 4096], P(None, 'row', 'col')
- child_block: float32 [2, 4096, 4096], P(None, 'row', 'col')
Inputs may be any that keep to these rules, and one draw needn't show every extreme that they name: `root_inverse`: lower triangular with a positive diagonal. `child_inverse`: each child's matrix is lower triangular with a positive diagonal. `ancestors`: each row holds 8 distinct block numbers in increasing order; the first is 0 and the last 63.
All inputs are finite; a program needn't handle non-finite values.
Results may differ from a plain program's by a relative error of at most 0.0048.
Values may be sent and summed in bfloat16 or wider, within the bound.
No kernel may reach another device: no remote copies, remote signals or barrier semaphores. Data moves between devices by JAX's collectives and lax.ppermute only.
A program may use at most 192 MiB of HBM per device.

v0:
```python
import jax
import jax.numpy as jnp
from jax import lax
from jax.sharding import PartitionSpec as P

BLOCK = 128


def column_panel(shard_part):
    return lax.all_gather(shard_part, "row", axis=1, tiled=True)


def band_total(partial_value):
    return lax.psum_scatter(partial_value, "row", scatter_dimension=1, tiled=True)


def gram_reduce(left_part, right_part):
    partial_value = jnp.einsum(
        "bkm,bkn->bmn",
        lax.all_gather(left_part, "col", axis=2, tiled=True),
        right_part,
        preferred_element_type=jnp.float32,
    )
    return band_total(partial_value)


def ancestor_rows(ancestors):
    within = jnp.arange(BLOCK, dtype=jnp.int32)
    return (ancestors[:, :, None] * BLOCK + within[None, None, :]).reshape(ancestors.shape[0], -1)


def take_columns(matrix, indices):
    return jnp.take(matrix, indices, axis=1)


def shards(root_inverse, child_inverse, child_panel, ancestors):
    root_batch = root_inverse[None]
    root_block = gram_reduce(root_batch, root_batch)[0]
    band_rows, band_cols = root_block.shape
    global_rows = ancestor_rows(ancestors)
    row_local = global_rows - lax.axis_index("row") * band_rows
    row_inside = (row_local >= 0) & (row_local < band_rows)
    picked = jnp.take(root_block, jnp.clip(row_local, 0, band_rows - 1), axis=0)
    picked = jnp.where(row_inside[:, :, None], picked, 0.0)
    own_rows = band_total(picked)
    col_local = global_rows - lax.axis_index("col") * band_cols
    col_inside = (col_local >= 0) & (col_local < band_cols)
    chosen = jax.vmap(take_columns)(own_rows, jnp.clip(col_local, 0, band_cols - 1))
    chosen = jnp.where(col_inside[:, None, :], chosen, 0.0)
    ancestor_block = lax.psum(chosen.astype(jnp.bfloat16), "col")
    child_cols = column_panel(child_inverse)
    update = jnp.einsum(
        "bak,bkn->ban",
        lax.all_gather(child_panel, "col", axis=2, tiled=True),
        child_cols,
        preferred_element_type=jnp.float32,
    ).astype(jnp.bfloat16)
    update_cols = column_panel(update)
    coupled = jnp.einsum(
        "bai,bin->ban", ancestor_block, update_cols, preferred_element_type=jnp.float32
    )
    cross_block = -coupled
    coupled_half = coupled.astype(jnp.bfloat16)
    left_stack = jnp.concatenate([child_inverse, update], axis=1)
    right_stack = jnp.concatenate([child_inverse, coupled_half], axis=1)
    child_block = gram_reduce(left_stack, right_stack)
    return (root_block, cross_block, child_block)


def solution(mesh):
    in_specs = (P("row", "col"), P(None, "row", "col"), P(None, "row", "col"), P())
    out_specs = (P("row", "col"), P(None, "row", "col"), P(None, "row", "col"))
    return jax.shard_map(shards, mesh=mesh, in_specs=in_specs, out_specs=out_specs, check_vma=False)
```

profile of v0, /device:TPU:4, one launch (start us, length us, event | category | flops | bytes accessed | tf_op | source)
XLA Modules:
  0.0 697.6 jit_solution(16673732814300745927)
XLA Ops:
  7.2 0.7 all-gather.12.cloned.1.call-update
  7.9 154.6 %all-gather.12.cloned.1.call-done = bf16[1024,8192]{1,0:T(8,128)(2,1)} async-done(((bf16[1024,256]{1,0:T(8,128)(2,1)}), bf16[1024,8192]{1,0:T(8,128)(2,1)}) %all-gather.12.cloned.1.call-update) | async-done | bytes 16777232 | tf_op jit(solution)/shard_map/all_gather | solution.py:20
  162.5 13.8 %convolution_bitcast_fusion = f32[1,8192,256]{2,1,0:T(8,128)} fusion(bf16[1024,8192]{1,0:T(8,128)(2,1)} %all-gather.12.cloned.1.call-done, bf16[1024,256]{1,0:T(8,128)(2,1)} %param.4), kind=kOutput, calls=%fused_computation.2 | convolution fusion | flops 4294967296 | bytes 25690112 | tf_op jit(solution)/shard_map/bkm,bkn->bmn/dot_general | solution.py:18
  176.4 0.6 copy-done.1
  177.3 52.7 %reduce-scatter.4.cloned.1.call-done = f32[1,1024,256]{2,1,0:T(8,128)} async-done(((f32[1,8192,256]{2,1,0:T(8,128)}), f32[1,1024,256]{2,1,0:T(8,128)}) %reduce-scatter.4.cloned.1.call-update) | async-done | bytes 1048592 | tf_op jit(solution)/shard_map/reduce_scatter | solution.py:14
  229.9 7.9 %gather_fusion = f32[2048,256]{1,0:T(8,128)S(1)} fusion(f32[1024,256]{1,0:T(8,128)} %bitcast.39, s32[2048]{0:T(1024)S(1)} %bitcast_clamp_fusion), kind=kCustom, calls=%fused_computation | custom fusion | bytes 4202496 | tf_op jit(solution)/shard_map/jit(_take)/gather | solution.py:43
  237.8 1.9 copy.10
  239.7 3.4 select_select_fusion
  243.1 0.5 all-gather.8.cloned.1.call-update
  243.7 0.5 all-gather.6.cloned.1.call-update
  244.3 34.7 %reduce-scatter.6.cloned.1.call-done = f32[2,128,256]{1,2,0:T(8,128)} async-done(((f32[2,1024,256]{1,2,0:T(8,128)}), f32[2,128,256]{1,2,0:T(8,128)}) %reduce-scatter.6.cloned.1.call-update) | async-done | bytes 262160 | tf_op jit(solution)/shard_map/reduce_scatter | solution.py:14
  279.0 8.5 %gather_fusion.1 = bf16[2048,128]{1,0:T(8,128)(2,1)S(1)} fusion(f32[2,128,256]{1,2,0:T(8,128)} %reduce-scatter.6.cloned.1.call-done, s32[2048]{0:T(1024)S(1)} %bitcast.41), kind=kCustom, calls=%fused_computation.1 | custom fusion | bytes 1064960 | tf_op jit(solution)/shard_map/vmap(jit(_take))/gather | solution.py:33
  287.5 0.2 copy.11
  287.8 0.9 fusion
  288.9 18.3 %all-gather.8.cloned.1.call-done = bf16[2,4096,128]{2,1,0:T(8,128)(2,1)} async-done(((bf16[2,512,128]{2,1,0:T(8,128)(2,1)}), bf16[2,4096,128]{2,1,0:T(8,128)(2,1)}) %all-gather.8.cloned.1.call-update) | async-done | bytes 2097168 | tf_op jit(solution)/shard_map/all_gather | solution.py:10
  307.3 77.6 %all-gather.6.cloned.1.call-done = bf16[2,128,4096]{2,1,0:T(8,128)(2,1)} async-done(((bf16[2,128,128]{2,1,0:T(8,128)(2,1)}), bf16[2,128,4096]{2,1,0:T(8,128)(2,1)}) %all-gather.6.cloned.1.call-update) | async-done | bytes 2097168 | tf_op jit(solution)/shard_map/all_gather | solution.py:54
  384.9 2.9 convolution_convert_fusion
  387.9 0.8 pad_maximum_fusion
  388.7 13.6 %all_gather.18 = bf16[2,1024,128]{2,1,0:T(8,128)(2,1)S(1)} all-gather(bf16[2,128,128]{2,1,0:T(8,128)(2,1)S(1)} %convolution_convert_fusion), channel_id=1, replica_groups=mesh['row'=8,'col'=32] {'row'}, dimensions={1}, use_global_device_ids=true | all-gather | bytes 589824 | tf_op jit(solution)/shard_map/all_gather | solution.py:10
  402.4 131.4 %all-reduce.2.cloned.1.call-done = bf16[2,128,1024]{2,1,0:T(8,128)(2,1)} async-done(((bf16[2,128,1024]{2,1,0:T(8,128)(2,1)}), bf16[2,128,1024]{2,1,0:T(8,128)(2,1)}) %all-reduce.2.cloned.1.call-update) | async-done | bytes 524304 | tf_op jit(solution)/shard_map/psum | solution.py:50
  533.8 2.0 fusion.11
  535.8 106.8 %all-gather.10.cloned.1.call-done = bf16[2,640,4096]{1,2,0:T(8,128)(2,1)} async-done(((bf16[2,640,128]{1,2,0:T(8,128)(2,1)}), bf16[2,640,4096]{1,2,0:T(8,128)(2,1)}) %all-gather.10.cloned.1.call-update) | async-done | bytes 10485776 | tf_op jit(solution)/shard_map/all_gather | solution.py:20
  642.6 8.9 %fusion.1 = f32[2,4096,128]{2,1,0:T(8,128)} fusion(bf16[2,640,4096]{1,2,0:T(8,128)(2,1)} %all-gather.10.cloned.1.call-done, bf16[2,128,128]{2,1,0:T(8,128)(2,1)S(1)} %get-tuple-element.3, bf16[2,512,128]{2,1,0:T(8,128)(2,1)S(1)} %copy-done), kind=kOutput, calls=%fused_computation.8 | convolution fusion | flops 1342832640 | bytes 15007744 | tf_op jit(solution)/shard_map/bkm,bkn->bmn/dot_general | solution.py:18
  651.5 39.2 %reduce-scatter.8.cloned.1.call-done = f32[2,512,128]{2,1,0:T(8,128)} async-done(((f32[2,4096,128]{2,1,0:T(8,128)}), f32[2,512,128]{2,1,0:T(8,128)}) %reduce-scatter.8.cloned.1.call-update) | async-done | bytes 524304 | tf_op jit(solution)/shard_map/reduce_scatter | solution.py:14
  (27 shorter events, 0.9 us)
Async XLA Ops:
  7.2 155.4 %all-gather.12.cloned.1.call-start = ((), (), s32[]{:S(2)}) async-start(), calls=%async_computation.10 | async-start | bytes 17301504 | tf_op jit(solution)/shard_map/all_gather | solution.py:20
  7.9 222.0 %reduce-scatter.4.cloned.1.call-start = ((), (), s32[]{:S(2)}) async-start(), calls=%async_computation.3 | async-start | bytes 9437184 | tf_op jit(solution)/shard_map/reduce_scatter | solution.py:14
  176.3 0.7 copy-start.1
  176.3 102.7 %reduce-scatter.6.cloned.1.call-start = ((), (), s32[]{:S(2)}) async-start(), calls=%async_computation.4 | async-start | bytes 2359296 | tf_op jit(solution)/shard_map/reduce_scatter | solution.py:14
  243.1 64.2 %all-gather.8.cloned.1.call-start = ((), (), s32[]{:S(2)}) async-start(), calls=%async_computation.7 | async-start | bytes 2359296 | tf_op jit(solution)/shard_map/all_gather | solution.py:10
  243.6 141.2 %all-gather.6.cloned.1.call-start = ((), (), s32[]{:S(2)}) async-start(), calls=%async_computation.6 | async-start | bytes 2162688 | tf_op jit(solution)/shard_map/all_gather | solution.py:54
  244.2 289.6 %all-reduce.2.cloned.1.call-start = ((), (), s32[]{:S(2)}) async-start(), calls=%async_computation.5 | async-start | bytes 1048576 | tf_op jit(solution)/shard_map/psum | solution.py:50
  287.5 1.3 copy-start
  288.7 353.8 %all-gather.10.cloned.1.call-start = ((), (), s32[]{:S(2)}) async-start(), calls=%async_computation.8 | async-start | bytes 10813440 | tf_op jit(solution)/shard_map/all_gather | solution.py:20
  388.7 302.0 %reduce-scatter.8.cloned.1.call-start = ((), (), s32[]{:S(2)}) async-start(), calls=%async_computation.9 | async-start | bytes 4718592 | tf_op jit(solution)/shard_map/reduce_scatter | solution.py:14
Sparse Core Ops, SparseCore 0:
  10.5 152.0 all-gather.11
  176.5 53.4 reduce-scatter.3
  243.2 35.7 reduce-scatter.5
  280.7 26.5 all-gather.7
  309.6 75.2 all-gather.5
  388.7 145.0 all-reduce.1
  536.7 105.8 all-gather.9
  651.6 39.0 reduce-scatter.7
where the time goes:
time: 698 us
  waiting for transfers between devices  617 us (88%)
  matrix products  27.6 us (4%)
  local copies, waits for them, and re-layouts  19.5 us (3%)
  between operations  14.2 us (2%)
  blocking collectives  13.6 us (2%)
    all_gather x2, waiting for transfers between devices, gram_reduce(): lax.all_gather(left_part, 'col', axis=2, tiled=True)  261 us
    psum x1, waiting for transfers between devices, shards(): ancestor_block = lax.psum(chosen.astype(jnp.bfloat16), 'col')  131 us
    reduce_scatter x3, waiting for transfers between devices, band_total(): lax.psum_scatter(partial_value, 'row', scatter_dimension=1, tiled=True)  127 us
    all_gather x1, waiting for transfers between devices, shards(): lax.all_gather(child_panel, 'col', axis=2, tiled=True)  77.6 us
    dot_general x2, matrix products, gram_reduce(): jnp.einsum('bkm,bkn->bmn', lax.all_gather(left_part, 'col', axis=2, tiled...  22.7 us
    all_gather x1, waiting for transfers between devices, column_panel(): return lax.all_gather(shard_part, 'row', axis=1, tiled=True)  18.3 us
  transfers between devices with their start and end apart: 8, of which 8 were waited for; matrix products, arithmetic and copies ran while one was open for 2% of the time, Pallas kernels for 0%

commit v1 on v0

--- a/solution.py
+++ b/solution.py
@@ -17,7 +17,9 @@
 def gram_reduce(left_part, right_part):
     partial_value = jnp.einsum(
         "bkm,bkn->bmn",
-        lax.all_gather(left_part, "col", axis=2, tiled=True),
+        jnp.concatenate(
+            lax.all_to_all(jnp.stack([left_part] * lax.axis_size("col")), "col", 0, 0), axis=2
+        ),
         right_part,
         preferred_element_type=jnp.float32,
     )

time: 698 us -> 841 us (1.20)
  waiting for transfers between devices: 617 us -> 720 us
  local copies, waits for them, and re-layouts: 19.5 us -> 41 us
  starting transfers between devices: 0.32 us -> 20.5 us
    all_to_all x0 -> x2, waiting for transfers between devices: none -> 526 us  [gram_reduce(): lax.all_to_all(jnp.stack([left_part] * lax.axis_size('col')), 'col', 0, 0)]
    all_gather x2 -> x0, waiting for transfers between devices: 261 us -> none  [gram_reduce(): lax.all_gather(left_part, 'col', axis=2, tiled=True)]
    all_gather x1, waiting for transfers between devices: 77.6 us -> 0.02 us  [shards(): lax.all_gather(child_panel, 'col', axis=2, tiled=True)]
    psum x1, waiting for transfers between devices: 131 us -> 77.5 us  [shards(): ancestor_block = lax.psum(chosen.astype(jnp.bfloat16), 'col')]
    all_to_all x0 -> x2, starting transfers between devices: none -> 20.2 us  [gram_reduce(): lax.all_to_all(jnp.stack([left_part] * lax.axis_size('col')), 'col', 0, 0)]
    all_gather x1, waiting for transfers between devices: 18.3 us -> 0.02 us  [column_panel(): return lax.all_gather(shard_part, 'row', axis=1, tiled=True)]
    reduce_scatter x3, waiting for transfers between devices: 127 us -> 115 us  [band_total(): lax.psum_scatter(partial_value, 'row', scatter_dimension=1, tiled=True)]
    another operation x0 -> x2, local copies, waits for them, and re-layouts: none -> 11.4 us  [gram_reduce(): jnp.stack([left_part] * lax.axis_size('col'))]
  transfers between devices with their start and end apart: 8 -> 8, of which waited for: 8 -> 6; matrix products, arithmetic and copies ran while one was open for 2% -> 7% of each run, Pallas kernels for 0% -> 0%
where the time goes in v1:
time: 841 us; the launch traced here: 840 us
  waiting for transfers between devices  720 us (86%)
  local copies, waits for them, and re-layouts  41 us (5%)
  matrix products  27.3 us (3%)
  starting transfers between devices  20.5 us (2%)
  between operations  14.3 us (2%)
  blocking collectives  13.3 us (2%)
    all_to_all x2, waiting for transfers between devices, gram_reduce(): lax.all_to_all(jnp.stack([left_part] * lax.axis_size('col')), 'col', 0, 0)  526 us
    reduce_scatter x3, waiting for transfers between devices, band_total(): lax.psum_scatter(partial_value, 'row', scatter_dimension=1, tiled=True)  115 us
    psum x1, waiting for transfers between devices, shards(): ancestor_block = lax.psum(chosen.astype(jnp.bfloat16), 'col')  77.5 us
    dot_general x2, matrix products, gram_reduce(): jnp.einsum('bkm,bkn->bmn', jnp.concatenate(lax.all_to_all(jnp.stack([left...  22.4 us
    all_to_all x2, starting transfers between devices, gram_reduce(): lax.all_to_all(jnp.stack([left_part] * lax.axis_size('col')), 'col', 0, 0)  20.2 us
  transfers between devices with their start and end apart: 8, of which 6 were waited for; matrix products, arithmetic and copies ran while one was open for 7% of the time, Pallas kernels for 0%

profile of v1, /device:TPU:4, one launch (start us, length us, event | category | flops | bytes accessed | tf_op | source)
XLA Modules:
  0.0 840.4 jit_solution(173485470885616809)
XLA Ops:
  7.2 1.2 copy.13
  8.4 6.0 stack.4
  14.5 11.8 %all-to-all-start = ((bf16[32,1,1024,256]{2,3,1,0:T(8,128)(2,1)}), bf16[32,1,1024,256]{2,3,1,0:T(8,128)(2,1)}, u32[]{:S(2)}, u32[]{:S(2)}) async-start(bf16[32,1,1024,256]{2,3,1,0:T(8,128)(2,1)} %stack.4), calls=%async_computation | async-start | bytes 33554432 | tf_op jit(solution)/shard_map/all_to_all | solution.py:21
  26.3 0.7 all-gather.5.cloned.1.call-update
  27.0 0.7 all-gather.3.cloned.1.call-update
  27.8 407.5 %all-to-all-done = bf16[32,1,1024,256]{2,3,1,0:T(8,128)(2,1)} async-done(((bf16[32,1,1024,256]{2,3,1,0:T(8,128)(2,1)}), bf16[32,1,1024,256]{2,3,1,0:T(8,128)(2,1)}, u32[]{:S(2)}, u32[]{:S(2)}) %all-to-all-start) | async-done | bytes 16777248 | tf_op jit(solution)/shard_map/all_to_all | solution.py:21
  435.2 13.6 %convolution_bitcast_fusion = f32[1,8192,256]{2,1,0:T(8,128)} fusion(bf16[1024,8192]{0,1:T(8,128)(2,1)} %bitcast.2, bf16[1024,256]{1,0:T(8,128)(2,1)S(1)} %copy-done.1), kind=kOutput, calls=%fused_computation.2 | convolution fusion | flops 4294967296 | bytes 25690112 | tf_op jit(solution)/shard_map/bkm,bkn->bmn/dot_general | solution.py:18
  448.9 2.9 convolution_convert_fusion
  452.1 5.4 stack.5
  457.5 8.5 %all-to-all-start.1 = ((bf16[32,2,640,128]{2,3,1,0:T(8,128)(2,1)}), bf16[32,2,640,128]{2,3,1,0:T(8,128)(2,1)}, u32[]{:S(2)}, u32[]{:S(2)}) async-start(bf16[32,2,640,128]{2,3,1,0:T(8,128)(2,1)} %stack.5), calls=%async_computation.3 | async-start | bytes 20971520 | tf_op jit(solution)/shard_map/all_to_all | solution.py:21
  466.3 38.5 %reduce-scatter.4.cloned.1.call-done = f32[1,1024,256]{2,1,0:T(8,128)} async-done(((f32[1,8192,256]{2,1,0:T(8,128)}), f32[1,1024,256]{2,1,0:T(8,128)}) %reduce-scatter.4.cloned.1.call-update) | async-done | bytes 1048592 | tf_op jit(solution)/shard_map/reduce_scatter | solution.py:14
  504.8 7.9 gather_fusion
  512.7 1.9 copy.15
  514.6 3.4 select_select_fusion
  518.0 37.1 %reduce-scatter.6.cloned.1.call-done = f32[2,128,256]{1,2,0:T(8,128)} async-done(((f32[2,1024,256]{1,2,0:T(8,128)}), f32[2,128,256]{1,2,0:T(8,128)}) %reduce-scatter.6.cloned.1.call-update) | async-done | bytes 262160 | tf_op jit(solution)/shard_map/reduce_scatter | solution.py:14
  555.1 8.5 %gather_fusion.1 = bf16[2048,128]{1,0:T(8,128)(2,1)S(1)} fusion(f32[2,128,256]{1,2,0:T(8,128)} %reduce-scatter.6.cloned.1.call-done, s32[2048]{0:T(1024)S(1)} %bitcast.48), kind=kCustom, calls=%fused_computation.1 | custom fusion | bytes 1064960 | tf_op jit(solution)/shard_map/vmap(jit(_take))/gather | solution.py:35
  563.8 0.9 fusion
  564.8 13.3 %all_gather.11 = bf16[2,1024,128]{2,1,0:T(8,128)(2,1)S(1)} all-gather(bf16[2,128,128]{2,1,0:T(8,128)(2,1)S(1)} %convolution_convert_fusion), channel_id=1, replica_groups=mesh['row'=8,'col'=32] {'row'}, dimensions={1}, use_global_device_ids=true | all-gather | bytes 589824 | tf_op jit(solution)/shard_map/all_gather | solution.py:10
  578.1 118.6 %all-to-all-done.1 = bf16[32,2,640,128]{2,3,1,0:T(8,128)(2,1)} async-done(((bf16[32,2,640,128]{2,3,1,0:T(8,128)(2,1)}), bf16[32,2,640,128]{2,3,1,0:T(8,128)(2,1)}, u32[]{:S(2)}, u32[]{:S(2)}) %all-to-all-start.1) | async-done | bytes 10485792 | tf_op jit(solution)/shard_map/all_to_all | solution.py:21
  696.8 9.5 %copy.18 = bf16[2,640,32,128]{1,3,2,0:T(8,128)(2,1)} copy(bf16[2,640,32,128]{1,3,0,2:T(8,128)(2,1)} %bitcast.9) | data formatting | bytes 20971520 | tf_op jit(solution)/shard_map/reshape | solution.py:20
  706.3 77.5 %all-reduce.2.cloned.1.call-done = bf16[2,128,1024]{2,1,0:T(8,128)(2,1)} async-done(((bf16[2,128,1024]{2,1,0:T(8,128)(2,1)}), bf16[2,128,1024]{2,1,0:T(8,128)(2,1)}) %all-reduce.2.cloned.1.call-update) | async-done | bytes 524304 | tf_op jit(solution)/shard_map/psum | solution.py:52
  783.7 2.0 fusion.11
  785.7 8.8 %fusion.1 = f32[2,4096,128]{2,1,0:T(8,128)} fusion(bf16[2,640,4096]{1,2,0:T(8,128)(2,1)} %bitcast.49, bf16[2,128,128]{2,1,0:T(8,128)(2,1)S(1)} %get-tuple-element.3, bf16[2,512,128]{2,1,0:T(8,128)(2,1)S(1)} %copy-done), kind=kOutput, calls=%fused_computation.8 | convolution fusion | flops 1342832640 | bytes 15007744 | tf_op jit(solution)/shard_map/bkm,bkn->bmn/dot_general | solution.py:18
  794.6 38.9 %reduce-scatter.8.cloned.1.call-done = f32[2,512,128]{2,1,0:T(8,128)} async-done(((f32[2,4096,128]{2,1,0:T(8,128)}), f32[2,512,128]{2,1,0:T(8,128)}) %reduce-scatter.8.cloned.1.call-update) | async-done | bytes 524304 | tf_op jit(solution)/shard_map/reduce_scatter | solution.py:14
  (30 shorter events, 1.1 us)
Async XLA Ops:
  14.4 420.8 %copy-start.1 = (bf16[1024,256]{1,0:T(8,128)(2,1)S(1)}, bf16[1024,256]{1,0:T(8,128)(2,1)}, u32[]{:S(2)}) copy-start(bf16[1024,256]{1,0:T(8,128)(2,1)} %param.4) | copy-start | bytes 1572868
  14.5 420.8 %all-to-all-start = ((bf16[32,1,1024,256]{2,3,1,0:T(8,128)(2,1)}), bf16[32,1,1024,256]{2,3,1,0:T(8,128)(2,1)}, u32[]{:S(2)}, u32[]{:S(2)}) async-start(bf16[32,1,1024,256]{2,3,1,0:T(8,128)(2,1)} %stack.4), calls=%async_computation | async-start | bytes 33554432 | tf_op jit(solution)/shard_map/all_to_all | solution.py:21
  26.2 422.6 %all-gather.5.cloned.1.call-start = ((), (), s32[]{:S(2)}) async-start(), calls=%async_computation.9 | async-start | bytes 2359296 | tf_op jit(solution)/shard_map/all_gather | solution.py:10
  27.0 421.9 %all-gather.3.cloned.1.call-start = ((), (), s32[]{:S(2)}) async-start(), calls=%async_computation.8 | async-start | bytes 2162688 | tf_op jit(solution)/shard_map/all_gather | solution.py:56
  27.7 477.1 %reduce-scatter.4.cloned.1.call-start = ((), (), s32[]{:S(2)}) async-start(), calls=%async_computation.5 | async-start | bytes 9437184 | tf_op jit(solution)/shard_map/reduce_scatter | solution.py:14
  448.8 3.0 copy-start
  457.5 8.5 %copy-start.2 = (s32[2,8]{1,0:T(2,128)S(1)}, s32[2,8]{1,0:T(2,128)}, u32[]{:S(2)}) copy-start(s32[2,8]{1,0:T(2,128)} %param.7) | copy-start | bytes 196
  457.5 239.3 %all-to-all-start.1 = ((bf16[32,2,640,128]{2,3,1,0:T(8,128)(2,1)}), bf16[32,2,640,128]{2,3,1,0:T(8,128)(2,1)}, u32[]{:S(2)}, u32[]{:S(2)}) async-start(bf16[32,2,640,128]{2,3,1,0:T(8,128)(2,1)} %stack.5), calls=%async_computation.3 | async-start | bytes 20971520 | tf_op jit(solution)/shard_map/all_to_all | solution.py:21
  466.0 89.1 %reduce-scatter.6.cloned.1.call-start = ((), (), s32[]{:S(2)}) async-start(), calls=%async_computation.6 | async-start | bytes 2359296 | tf_op jit(solution)/shard_map/reduce_scatter | solution.py:14
  518.0 265.8 %all-reduce.2.cloned.1.call-start = ((), (), s32[]{:S(2)}) async-start(), calls=%async_computation.7 | async-start | bytes 1048576 | tf_op jit(solution)/shard_map/psum | solution.py:52
  564.8 268.7 %reduce-scatter.8.cloned.1.call-start = ((), (), s32[]{:S(2)}) async-start(), calls=%async_computation.10 | async-start | bytes 4718592 | tf_op jit(solution)/shard_map/reduce_scatter | solution.py:14
Sparse Core Ops, SparseCore 0:
  28.9 28.8 all-gather.4
  60.3 230.2 all-gather.2
  449.0 55.8 reduce-scatter.3
  518.1 36.9 reduce-scatter.5
  564.9 218.7 all-reduce.1
  794.7 38.7 reduce-scatter.7
